TPU v7x, 32 devices: a whole 2x2x4 slice. The times are simulated.
32 devices in a mesh: day: 2 (over y), tile: 4 (over z), freq: 2 (over x), sub: 2 (over core).
Axes of the slice: x: 2, y: 2, z: 4, core: 2. Of those that a mesh axis runs over, the one named last changes fastest.
Arguments:
- spectra: float32 [4, 16, 256, 1024], P('day', None, 'freq', ('tile', 'sub')), parts along dimension 0, may hold values from -6 to 6
- pair_list: int32 [6, 2], replicated, may hold values from 0 to 7, as said below
- owner_slots: int32 [4, 2], replicated, may hold values from -1 to 5, as said below
Outputs:
- lagged: float32 [128, 16, 256, 128], P(('sub', 'freq'), ('day', 'tile')), parts along dimension 1
There are 2 independent parts, one for each index of `day`. A program takes and returns all parts, laid end to end along the dimension named above; an argument that names none is the same for every part. Nothing has to cross between parts.
Inputs may be any that keep to these rules, and one draw needn't show every extreme that they name: `pair_list`: each row names a block and then a block 0 to 3 further along; the first row starts at block 0 and the last row starts at the last block. `owner_slots`: every pair number appears exactly once; -1 marks an empty slot; some owner has all 2 slots filled.
All inputs are finite; a program needn't handle non-finite values.
Results may differ from a plain program's by a relative error of at most 0.0003.
Values sent between devices are 32-bit elements; how exact they have to be, the bound alone decides.
No kernel may reach another device: no remote copies, remote signals or barrier semaphores. Data moves between devices by JAX's collectives and lax.ppermute only.
A program may use at most 128 MiB of HBM per device.

v0:
```python
import math

import jax
import jax.numpy as jnp
from jax import lax
from jax.sharding import PartitionSpec as P

FREQS = 256
LAGS = 256


def whiten(spectra):
    amplitude = jnp.sqrt(spectra[0] * spectra[0] + spectra[1] * spectra[1])
    return spectra / jnp.maximum(amplitude, 1.0)


def lag_table(freq_start, freq_count, total_freq, lag_count):
    freq_ids = freq_start + lax.iota(jnp.int32, freq_count)
    lag_ids = lax.iota(jnp.int32, lag_count) - lag_count // 2
    phases = lag_ids[:, None] * freq_ids[None, :] % (2 * total_freq)
    angles = phases.astype(jnp.float32) * (jnp.pi / total_freq)
    norm_scale = 1.0 / math.sqrt(total_freq)
    return jnp.concatenate([jnp.cos(angles), -jnp.sin(angles)], axis=1) * norm_scale


def body(spectra, pair_list, owner_slots):
    tile_count = lax.axis_size("tile")
    halves = lax.axis_size("sub")
    windows = spectra.shape[1]
    band_count = spectra.shape[2]
    block_width = spectra.shape[3]
    row_width = block_width // halves
    slot_count = owner_slots.shape[1]
    whitened = whiten(spectra)
    spread_out = lax.all_to_all(whitened, "tile", split_axis=2, concat_axis=3, tiled=True)
    everyone = lax.all_gather(spread_out, "sub", axis=3, tiled=True)
    local_freqs = everyone.shape[2]
    blocks = everyone.reshape(2, windows, local_freqs, halves * tile_count, block_width)
    first_pos = pair_list[:, 0] % halves * tile_count + pair_list[:, 0] // halves
    second_pos = pair_list[:, 1] % halves * tile_count + pair_list[:, 1] // halves
    row_part = jnp.take(blocks, first_pos, axis=3)
    row_part = lax.dynamic_slice_in_dim(row_part, lax.axis_index("sub") * row_width, row_width, 4)
    col_part = jnp.take(blocks, second_pos, axis=3)
    turned = jnp.stack([row_part[1], -row_part[0]])
    stacked_rows = jnp.stack([row_part, turned])
    cross_spec = jnp.einsum(
        "ekwfpr,kwfpc->pefrc", stacked_rows, col_part, precision=lax.Precision.HIGHEST
    )
    cross_spec = cross_spec / math.sqrt(windows)
    filled = (owner_slots >= 0).astype(jnp.float32)
    outgoing = jnp.take(cross_spec, jnp.maximum(owner_slots, 0).reshape(-1), axis=0)
    outgoing = outgoing.reshape(tile_count, slot_count, 2, local_freqs, row_width, block_width)
    outgoing = outgoing * filled.reshape(tile_count, slot_count, 1, 1, 1, 1)
    arrived = lax.all_to_all(outgoing, "tile", split_axis=0, concat_axis=3, tiled=True)
    arrived = arrived.reshape(slot_count, 2 * band_count, row_width, block_width)
    lag_weights = lag_table(lax.axis_index("freq") * band_count, band_count, FREQS, LAGS)
    return lax.psum_scatter(
        jnp.einsum("mq,kqrc->rkmc", lag_weights, arrived, precision=lax.Precision.HIGHEST),
        "freq",
        scatter_dimension=0,
        tiled=True,
    )


def solution(mesh):
    in_specs = (P("day", None, "freq", ("tile", "sub")), P(), P())
    out_specs = P(("sub", "freq"), ("day", "tile"), None, None)
    return jax.shard_map(body, mesh=mesh, in_specs=in_specs, out_specs=out_specs, check_vma=False)
```

profile of v0, /device:TPU:17, one launch (start us, length us, event | category | flops | bytes accessed | tf_op | source)
XLA Modules:
  0.0 818.4 jit_solution(17975509832532458652)
XLA Ops:
  6.5 2.1 maximum_bitcast_fusion.1
  10.5 49.8 %all_to_all.33 = f32[2,16,128,128]{3,1,0,2:T(8,128)S(1)} all-to-all(f32[2,16,128,128]{3,1,0,2:T(8,128)S(1)} %copy_divide_fusion), channel_id=1, replica_groups=mesh['day'=2,'tile'=4,'freq'=2,'sub'=2] {'tile'}, dimensions={2} | all-to-all | bytes 4194304 | tf_op jit(solution)/shard_map/all_to_all | solution.py:35
  60.3 1.4 copy.65
  61.7 1.8 all_to_all.27
  64.1 16.2 %all-gather.2.cloned.1.call-done = f32[2,16,32,1024]{3,2,1,0:T(8,128)} async-done(((f32[2,16,32,512]{3,2,1,0:T(8,128)}), f32[2,16,32,1024]{3,2,1,0:T(8,128)}) %all-gather.2.cloned.1.call-update) | async-done | bytes 4194320 | tf_op jit(solution)/shard_map/all_gather | solution.py:36
  80.3 4.7 copy_bitcast_fusion
  85.0 2.9 gather_fusion.2
  87.9 2.0 fusion.14
  89.9 2.5 dynamic-slice_bitcast_fusion
  92.4 2.5 constant_dynamic-slice_fusion
  94.9 2.9 gather_fusion.1
  97.9 2.2 maximum_bitcast_fusion
  102.0 22.8 %fusion.3 = f32[6,2,32,64,128]{4,3,1,2,0:T(8,128)} fusion(f32[1,2,16,32,6,64]{5,2,1,0,3,4:T(8,128)S(1)} %maximum_bitcast_fusion, f32[1,2,16,32,6,64]{5,2,1,0,3,4:T(8,128)S(1)} %copy-done, f32[2,16,32,6,128,1]{4,2,1,0,3,5:T(8,128)S(1)} %select_bitcast_fusion), kind=kOutput, calls=%fused_computation.8 | convolution fusion | flops 1211891712 | bytes 18874368 | tf_op jit(solution)/shard_map/ekwfpr,kwfpc->pefrc/dot_general | solution.py:46
  124.7 12.4 %gather_fusion = f32[8,2,32,64,128]{4,3,1,2,0:T(8,128)} fusion(f32[6,2,32,64,128]{4,3,1,2,0:T(8,128)} %fusion.3, s32[1024]{0:T(1024)S(1)} %pad_clamp_fusion), kind=kCustom, calls=%fused_computation.2 | custom fusion | bytes 33554464 | tf_op jit(solution)/shard_map/jit(_take)/gather | solution.py:51
  137.2 12.5 %fusion.2 = f32[4,2,2,32,64,128]{5,4,3,2,1,0:T(8,128)} fusion(f32[4,2,2,32,64,128]{5,4,2,3,1,0:T(8,128)} %bitcast.87, f32[4,2]{1,0:T(4,128)S(1)} %copy.35, pred[4,2]{1,0:T(4,128)(4,1)S(1)} %copy.25), kind=kLoop, calls=%fused_computation.6 | loop fusion | flops 8388608 | bytes 33554472 | tf_op jit(solution)/shard_map/mul | solution.py:53
  149.7 7.0 all-to-all-start.1
  157.3 359.1 %all-to-all-done.1 = f32[4,2,2,32,64,128]{5,4,3,2,1,0:T(8,128)} async-done(((f32[4,2,2,32,64,128]{5,4,3,2,1,0:T(8,128)}), f32[4,2,2,32,64,128]{5,4,3,2,1,0:T(8,128)}, u32[]{:S(2)}, u32[]{:S(2)}) %all-to-all-start.1) | async-done | bytes 16777248 | tf_op jit(solution)/shard_map/all_to_all | solution.py:54
  516.4 11.8 %copy.36 = f32[4,2,2,32,64,128]{5,4,3,0,2,1:T(8,128)} copy(f32[4,2,2,32,64,128]{5,4,3,2,1,0:T(8,128)} %all-to-all-done.1) | data formatting | bytes 33554432 | tf_op jit(solution)/shard_map/all_to_all | solution.py:54
  528.2 54.8 %fusion.4 = f32[64,2,256,128]{2,3,0,1:T(8,128)} fusion(f32[2,256,64,128]{3,2,1,0:T(8,128)} %bitcast.89, f32[256,128]{1,0:T(8,128)S(1)} %get-tuple-element.13, f32[256,128]{1,0:T(8,128)S(1)} %get-tuple-element.12), kind=kOutput, calls=%fused_computation.9 | convolution fusion | flops 12885032960 | bytes 33816576 | tf_op jit(solution)/shard_map/mq,kqrc->rkmc/dot_general | solution.py:58
  583.0 6.8 copy.44
  589.8 11.7 %copy.48 = f32[8,8,256,256]{3,1,2,0:T(8,128)} copy(f32[8,8,256,256]{3,2,1,0:T(8,128)S(1)} %bitcast.90) | data formatting | bytes 33554432
  601.5 191.7 %reduce-scatter.5.cloned.1.call-done = f32[32,65536]{1,0:T(8,128)} async-done(((f32[64,65536]{1,0:T(8,128)}), f32[32,65536]{1,0:T(8,128)}) %reduce-scatter.5.cloned.1.call-update) | async-done | bytes 8388624
  793.2 9.2 %copy.49 = f32[4,8,256,256]{3,2,1,0:T(8,128)} copy(f32[4,8,256,256]{3,1,2,0:T(8,128)} %bitcast.92) | data formatting | bytes 16777216
  802.4 8.9 %copy.38 = f32[32,2,256,128]{3,2,1,0:T(8,128)} copy(f32[32,2,256,128]{2,3,1,0:T(8,128)} %bitcast.91) | data formatting | bytes 16777216 | tf_op jit(solution)/shard_map/reduce_scatter | solution.py:57
  (28 shorter events, 4.9 us)
Async XLA Ops:
  6.5 2.7 copy-start.1
  6.5 73.7 %all-gather.2.cloned.1.call-start = ((), (), s32[]{:S(2)}) async-start(), calls=%async_computation.3 | async-start | bytes 6291456 | tf_op jit(solution)/shard_map/all_gather | solution.py:36
  61.7 1.9 copy-start.2
  61.7 2.3 copy-start.3
  100.1 1.9 copy-start
  149.7 366.8 %all-to-all-start.1 = ((f32[4,2,2,32,64,128]{5,4,3,2,1,0:T(8,128)}), f32[4,2,2,32,64,128]{5,4,3,2,1,0:T(8,128)}, u32[]{:S(2)}, u32[]{:S(2)}) async-start(f32[4,2,2,32,64,128]{5,4,3,2,1,0:T(8,128)} %fusion.2), calls=%async_computation.1 | async-start | bytes 33554432 | tf_op jit(solution)/shard_map/all_to_all | solution.py:54
  156.6 636.6 %reduce-scatter.5.cloned.1.call-start = ((), (), s32[]{:S(2)}) async-start(), calls=%async_computation.4 | async-start | bytes 25165824
Sparse Core Ops, SparseCore 0:
  63.7 16.5 all-gather.1
  601.6 191.5 reduce-scatter.4
where the time goes:
time: 822 us; the launch traced here: 818 us
  waiting for transfers between devices  567 us (69%)
  local copies, waits for them, and re-layouts  79.4 us (10%)
  matrix products  77.5 us (9%)
  blocking collectives  49.8 us (6%)
  other arithmetic  23.9 us (3%)
  between operations  13.8 us (2%)
    all_to_all x1, waiting for transfers between devices, body(): lax.all_to_all(outgoing, 'tile', split_axis=0, concat_axis=3, tiled=True)  359 us
    unnamed x3, waiting for transfers between devices  192 us
    dot_general x1, matrix products, body(): jnp.einsum('mq,kqrc->rkmc', lag_weights, arrived, precision=lax.Precision...  54.8 us
    all_to_all x1, blocking collectives, body(): lax.all_to_all(whitened, 'tile', split_axis=2, concat_axis=3, tiled=True)  49.8 us
    unnamed x11, local copies, waits for them, and re-layouts  28.9 us
    dot_general x1, matrix products, body(): jnp.einsum('ekwfpr,kwfpc->pefrc', stacked_rows, col_part, precision=lax.P...  22.8 us
  transfers between devices with their start and end apart: 3, of which 3 were waited for; matrix products, arithmetic and copies ran while one was open for 0% of the time, Pallas kernels for 0%

commit v1 on v0

v1 whole, which is shorter than its diff:
```python
import functools
import math

import jax
import jax.numpy as jnp
import ml_dtypes
import numpy as np
from jax import lax
from jax.experimental import pallas as pl
from jax.experimental.pallas import tpu as pltpu
from jax.sharding import PartitionSpec as P

FREQS = 256
LAGS = 256
BF16 = jnp.bfloat16
VMEM_LIMIT = 56 * 1024 * 1024


def lag_tables(scale):
    lag_ids = np.arange(LAGS) - LAGS // 2
    phases = (lag_ids[:, None] * np.arange(FREQS)[None, :]) % (2 * FREQS)
    angles = phases * (np.pi / FREQS)
    table = np.concatenate([np.cos(angles), -np.sin(angles)], axis=1) * scale
    head = table.astype(ml_dtypes.bfloat16)
    tail = (table - head.astype(np.float64)).astype(ml_dtypes.bfloat16)
    return np.concatenate([head, tail], axis=0)


def split(x):
    head = x.astype(BF16)
    return head, (x - head.astype(jnp.float32)).astype(BF16)


def whiten_kernel(part_ref, x_ref, o_ref):
    parts, windows, chunk, width = x_ref.shape
    for f in range(chunk):
        re = x_ref[0, :, f, :]
        im = x_ref[1, :, f, :]
        amplitude = jnp.maximum(jnp.sqrt(re * re + im * im), 1.0)
        o_ref[f, :windows, :] = re / amplitude
        o_ref[f, windows:, :] = im / amplitude


def whiten(spectra, part, fq):
    parts, windows, _, width = spectra.shape
    chunk = 16
    steps = fq // chunk
    return pl.pallas_call(
        whiten_kernel,
        grid_spec=pltpu.PrefetchScalarGridSpec(
            num_scalar_prefetch=1,
            grid=(steps,),
            in_specs=[pl.BlockSpec((parts, windows, chunk, width), lambda i, p: (0, 0, p[0] * steps + i, 0))],
            out_specs=pl.BlockSpec((chunk, parts * windows, width), lambda i, p: (i, 0, 0)),
        ),
        out_shape=jax.ShapeDtypeStruct((fq, parts * windows, width), jnp.float32),
        compiler_params=pltpu.CompilerParams(vmem_limit_bytes=VMEM_LIMIT),
        cost_estimate=pl.CostEstimate(flops=fq * 32 * width * 8, bytes_accessed=fq * 32 * width * 8, transcendentals=0),
        name="whiten",
    )(part.reshape(1), spectra)


def corr_kernel(nq, items, rows, slots, meta, *refs):
    srcs = refs[: nq * items]
    table, mask, out = refs[nq * items : nq * items + 3]
    row_buf, col_buf, cross, out_buf, in_sem, out_sem = refs[nq * items + 3 :]
    fq, kw, width = row_buf.shape[2:]
    group = 4
    packs = width // rows
    per_pack = group * packs
    m_rows = group * 2 * rows

    def fetch(slot):
        for which, buf in ((0, row_buf), (1, col_buf)):
            item = meta[1 + nq + 3 * slot + which]
            for q in range(nq):
                for n in range(items):

                    @pl.when(jnp.logical_and(item == n, meta[1 + nq + 3 * slot + 2] > 0))
                    def _():
                        pltpu.make_async_copy(srcs[q * items + n], buf.at[slot, q], in_sem.at[slot, which, q]).start()

    def wait_fetch(slot, q):
        for which, buf in ((0, row_buf), (1, col_buf)):
            pltpu.make_async_copy(srcs[0], buf.at[slot, q], in_sem.at[slot, which, q]).wait()

    def out_copy(slot, pair, buf):
        return pltpu.make_async_copy(out_buf.at[buf], out.at[pl.ds(pair * 2, 2), slot], out_sem.at[buf])

    for slot in range(slots):
        fetch(slot)

    lane = lax.broadcasted_iota(jnp.int32, (width, width), 1)
    for slot in range(slots):
        filled = meta[1 + nq + 3 * slot + 2] > 0

        @pl.when(filled)
        def _():
            for q in range(nq):
                wait_fetch(slot, q)

                @pl.loop(0, fq // per_pack)
                def _(p):
                    packed = jnp.zeros((width, width), jnp.float32)
                    for g in range(packs):
                        part = row_buf[slot, q, pl.ds(p * per_pack + g * group, group)].reshape(group * kw, width)
                        shift = lax.rem(meta[0] + g * rows, width)
                        packed = jnp.where(lane // rows == g, pltpu.roll(part, shift, 1), packed)
                    turned = packed.T
                    swapped = jnp.where(
                        lane % kw < kw // 2, pltpu.roll(turned, width - kw // 2, 1), -pltpu.roll(turned, kw // 2, 1)
                    )
                    for g in range(packs):
                        span = slice(g * rows, (g + 1) * rows)
                        head, tail = split(jnp.concatenate([turned[span], swapped[span]], axis=0))
                        left = jnp.concatenate(
                            [
                                jnp.concatenate([head * mask[n], tail * mask[n]], axis=1)
                                for n in range(group)
                            ],
                            axis=0,
                        )
                        part = col_buf[slot, q, pl.ds(p * per_pack + g * group, group)].reshape(group * kw, width)
                        top = jnp.concatenate(split(part), axis=1)
                        both = jnp.dot(left, jnp.concatenate([top, top], axis=0), preferred_element_type=jnp.float32)
                        first = (meta[1 + q] + p * per_pack + g * group) * (2 * rows)
                        cross[pl.ds(pl.multiple_of(first, m_rows), m_rows)] = both[:, :width] + both[:, width:]

        @pl.loop(0, rows // 2)
        def _(pair):
            buf = lax.rem(pair, 2)

            @pl.when(jnp.logical_or(pair >= 2, slot > 0))
            def _():
                out_copy(slot, pair, buf).wait()

            @pl.when(filled)
            def _():
                halves = [
                    jnp.concatenate(
                        [cross[pl.ds(e * rows + pair * 2 + n, FREQS, stride=2 * rows)] for n in range(2)], axis=1
                    )
                    for e in range(2)
                ]
                head, tail = split(jnp.concatenate(halves, axis=0))
                high = jnp.dot(table[...], head, preferred_element_type=jnp.float32)
                low = jnp.dot(table[:LAGS], tail, preferred_element_type=jnp.float32)
                lagged = high[:LAGS] + high[LAGS:] + low
                for n in range(2):
                    out_buf[buf, n] = lagged[:, n * width : (n + 1) * width]

            @pl.when(jnp.logical_not(filled))
            def _():
                out_buf[buf] = jnp.zeros(out_buf.shape[1:], jnp.float32)

            out_copy(slot, pair, buf).start()

    for buf in range(2):
        out_copy(0, 0, buf).wait()


def correlate(meta, srcs, rows, slots, windows):
    nq, items = len(srcs), len(srcs[0])
    fq, kw, width = srcs[0][0].shape
    table = jnp.asarray(lag_tables(1.0 / math.sqrt(windows * FREQS)))
    mask_np = np.broadcast_to((np.arange(width)[None, None, :] // kw) == np.arange(4)[:, None, None], (4, 2 * rows, width))
    mask = jnp.asarray(mask_np.astype(ml_dtypes.bfloat16))
    any_spec = pl.BlockSpec(memory_space=pl.ANY)
    vmem_spec = pl.BlockSpec(memory_space=pltpu.VMEM)
    return pl.pallas_call(
        functools.partial(corr_kernel, nq, items, rows, slots),
        in_specs=[pl.BlockSpec(memory_space=pltpu.SMEM)] + [any_spec] * (nq * items) + [vmem_spec] * 2,
        out_specs=any_spec,
        out_shape=jax.ShapeDtypeStruct((rows, slots, LAGS, width), jnp.float32),
        scratch_shapes=[
            pltpu.VMEM((slots, nq, fq, kw, width), jnp.float32),
            pltpu.VMEM((slots, nq, fq, kw, width), jnp.float32),
            pltpu.VMEM((FREQS * 2 * rows, width), jnp.float32),
            pltpu.VMEM((2, 2, LAGS, width), jnp.float32),
            pltpu.SemaphoreType.DMA((slots, 2, nq)),
            pltpu.SemaphoreType.DMA((2,)),
        ],
        compiler_params=pltpu.CompilerParams(vmem_limit_bytes=VMEM_LIMIT),
        name="correlate",
    )(meta, *[a for share in srcs for a in share], table, mask)


def body(spectra, pair_list, owner_slots):
    tiles = lax.axis_size("tile")
    freq_parts = lax.axis_size("freq")
    subs = lax.axis_size("sub")
    _, windows, band, width = spectra.shape
    slots = owner_slots.shape[1]
    nq = freq_parts * subs
    fq = band // subs
    rows = width // nq
    me_tile, me_freq, me_sub = lax.axis_index("tile"), lax.axis_index("freq"), lax.axis_index("sub")
    swap = [(0, 1), (1, 0)]
    other = whiten(spectra, 1 - me_sub, fq)
    passed = lax.ppermute(other, "sub", swap)
    mine = whiten(spectra, me_sub, fq)
    my_pairs = lax.dynamic_index_in_dim(owner_slots, me_tile, 0, keepdims=False)
    filled = (my_pairs >= 0).astype(jnp.int32)
    wanted = jnp.take(pair_list, jnp.maximum(my_pairs, 0), axis=0)
    shift = (width - (me_sub * freq_parts + me_freq) * rows) % width

    held = lax.all_gather(jnp.stack([mine, passed]), "tile")
    items = []
    for slot in range(slots):
        for which in range(2):
            block = wanted[slot, which]
            chosen = held[block // 2, (block % 2) ^ me_sub]
            items.append(lax.all_gather(chosen, ("freq", "sub")))
    srcs = [[item[q] for item in items] for q in range(nq)]
    first = jnp.arange(nq, dtype=jnp.int32) * fq
    meta = jnp.concatenate(
        [shift.reshape(1), first]
        + [jnp.stack([jnp.int32(2 * k), jnp.int32(2 * k + 1), filled[k]]) for k in range(slots)]
    ).astype(jnp.int32)
    return correlate(meta, srcs, rows, slots, windows)


def solution(mesh):
    in_specs = (P("day", None, "freq", ("tile", "sub")), P(), P())
    out_specs = P(("sub", "freq"), ("day", "tile"), None, None)
    return jax.shard_map(body, mesh=mesh, in_specs=in_specs, out_specs=out_specs, check_vma=False)
```

time: 822 us -> 371 us (0.45)
  waiting for transfers between devices: 567 us -> 264 us
  matrix products: 77.5 us -> 0 us
  local copies, waits for them, and re-layouts: 79.4 us -> 25 us
  Pallas kernels: 0 us -> 53 us
  blocking collectives: 49.8 us -> 0 us
  other arithmetic: 23.9 us -> 3.17 us
  between operations: 13.8 us -> 23.3 us
    all_to_all x1 -> x0, waiting for transfers between devices: 359 us -> none  [body(): lax.all_to_all(outgoing, 'tile', split_axis=0, concat_axis=3, tiled=True)]
    all_gather x1 -> x5, waiting for transfers between devices: 16.2 us -> 263 us  [the longest x1 137 us: body(): held = lax.all_gather(jnp.stack([mine, passed]), 'tile')]
    unnamed x3 -> x5, waiting for transfers between devices: 192 us -> 1.77 us
    dot_general x2 -> x0, matrix products: 77.5 us -> none  [the longest x1 54.8 us: body(): jnp.einsum('mq,kqrc->rkmc', lag_weights, arrived, precision=lax.Precision...]
    pallas_call x0 -> x3, Pallas kernels: none -> 53 us  [the longest x1 43.7 us: correlate(): pl.pallas_call(functools.partial(corr_kernel, nq, items, rows, slots), in...]
    all_to_all x1 -> x0, blocking collectives: 49.8 us -> none  [body(): lax.all_to_all(whitened, 'tile', split_axis=2, concat_axis=3, tiled=True)]
    unnamed x11 -> x5, local copies, waits for them, and re-layouts: 28.9 us -> 0.1 us
    gather x3 -> x1, local copies, waits for them, and re-layouts: 18.3 us -> 0.56 us  [body(): wanted = jnp.take(pair_list, jnp.maximum(my_pairs, 0), axis=0)]
  transfers between devices with their start and end apart: 3 -> 6, of which waited for: 3 -> 5; matrix products, arithmetic and copies ran while one was open for 0% -> 5% of each run, Pallas kernels for 0% -> 1%
where the time goes in v1:
time: 371 us; the launch traced here: 370 us
  waiting for transfers between devices  264 us (71%)
  Pallas kernels  53 us (14%)
  local copies, waits for them, and re-layouts  25 us (7%)
  between operations  23.3 us (6%)
    all_gather x1, waiting for transfers between devices, body(): held = lax.all_gather(jnp.stack([mine, passed]), 'tile')  137 us
    all_gather x4, waiting for transfers between devices, body(): items.append(lax.all_gather(chosen, ('freq', 'sub')))  126 us
    pallas_call x1, Pallas kernels, correlate(): pl.pallas_call(functools.partial(corr_kernel, nq, items, rows, slots), in...  43.7 us
    squeeze x4, local copies, waits for them, and re-layouts, body(): srcs = [[item[q] for item in items] for q in range(nq)]  16.9 us
    pallas_call x2, Pallas kernels, whiten(): pl.pallas_call(whiten_kernel, grid_spec=pltpu.PrefetchScalarGridSpec(num_...  9.3 us
  transfers between devices with their start and end apart: 6, of which 5 were waited for; matrix products, arithmetic and copies ran while one was open for 5% of the time, Pallas kernels for 1%

profile of v1, /device:TPU:17, one launch (start us, length us, event | category | flops | bytes accessed | tf_op | source)
XLA Modules:
  0.0 369.7 jit_solution(17174622304985416673)
XLA Ops:
  6.5 4.6 %whiten.3 = f32[64,32,128]{2,1,0:T(8,128)} custom-call(s32[1]{0:T(128)} %bitcast.5.part_ref, f32[2,16,128,128]{3,2,1,0:T(8,128)} %x_ref.3), custom_call_target="tpu_custom_call" | custom-call | flops 2097152 | bytes 2097152 | tf_op jit(solution)/shard_map/whiten/pallas_call | solution.py:48
  11.2 0.7 collective-permute-start
  11.9 4.7 %whiten.2 = f32[64,32,128]{2,1,0:T(8,128)} custom-call(s32[1]{0:T(128)} %bitcast.3.part_ref, f32[2,16,128,128]{3,2,1,0:T(8,128)} %x_ref.3), custom_call_target="tpu_custom_call" | custom-call | flops 2097152 | bytes 2097152 | tf_op jit(solution)/shard_map/whiten/pallas_call | solution.py:48
  16.5 2.7 pad_maximum_fusion
  19.4 0.2 maximum_reduce_fusion
  19.6 0.6 gather_fusion
  20.2 0.2 compare_reduce_fusion
  20.4 0.7 fusion
  31.2 136.6 %all-gather.11.cloned.1.call-done = f32[8,64,32,128]{3,2,1,0:T(8,128)} async-done(((f32[2,64,32,128]{3,2,1,0:T(8,128)}), f32[8,64,32,128]{3,2,1,0:T(8,128)}) %all-gather.11.cloned.1.call-update) | async-done | bytes 8388624 | tf_op jit(solution)/shard_map/all_gather | solution.py:207
  167.8 4.3 %constant_dynamic-slice_fusion = (f32[1,1,64,32,128]{4,3,2,1,0:T(8,128)}, f32[1,1,64,32,128]{4,3,2,1,0:T(8,128)}, f32[1,1,64,32,128]{4,3,2,1,0:T(8,128)}, f32[1,1,64,32,128]{4,3,2,1,0:T(8,128)}) fusion(f32[4,2,64,32,128]{4,3,2,1,0:T(8,128)} %bitcast.45, s32[]{:T(128)S(6)} %select_n.87, s32[]{:T(128)S(6)} %select_n.89, s32[]{:T(128)S(6)} %select_n.83, ...), kind=kLoop, calls=%fused_computation.21 | loop fusion | bytes 8388640 | tf_op jit(solution)/shard_map/dynamic_slice | solution.py:212
  172.2 0.7 all-gather.17.cloned.1.call-update
  172.9 0.5 all-gather.15.cloned.1.call-update
  173.5 0.5 all-gather.13.cloned.1.call-update
  174.1 0.5 fusion.1
  174.6 1.9 concatenate.3.meta
  176.5 30.8 %all-gather.19.cloned.1.call-done = f32[4,1,64,32,128]{4,3,2,1,0:T(8,128)} async-done(((f32[1,1,64,32,128]{4,3,2,1,0:T(8,128)}), f32[4,1,64,32,128]{4,3,2,1,0:T(8,128)}) %all-gather.19.cloned.1.call-update) | async-done | bytes 4194320 | tf_op jit(solution)/shard_map/all_gather | solution.py:213
  207.3 4.3 %slice_bitcast_fusion = (f32[64,32,128]{2,1,0:T(8,128)}, f32[64,32,128]{2,1,0:T(8,128)}, f32[64,32,128]{2,1,0:T(8,128)}, f32[64,32,128]{2,1,0:T(8,128)}) fusion(f32[4,1,64,32,128]{4,3,2,1,0:T(8,128)} %all-gather.19.cloned.1.call-done), kind=kLoop, calls=%fused_computation.2 | loop fusion | bytes 8388608 | tf_op jit(solution)/shard_map/squeeze | solution.py:214
  211.6 31.8 %all-gather.17.cloned.1.call-done = f32[4,1,64,32,128]{4,3,2,1,0:T(8,128)} async-done(((f32[1,1,64,32,128]{4,3,2,1,0:T(8,128)}), f32[4,1,64,32,128]{4,3,2,1,0:T(8,128)}) %all-gather.17.cloned.1.call-update) | async-done | bytes 4194320 | tf_op jit(solution)/shard_map/all_gather | solution.py:213
  243.4 4.2 %slice_bitcast_fusion.1 = (f32[64,32,128]{2,1,0:T(8,128)}, f32[64,32,128]{2,1,0:T(8,128)}, f32[64,32,128]{2,1,0:T(8,128)}, f32[64,32,128]{2,1,0:T(8,128)}) fusion(f32[4,1,64,32,128]{4,3,2,1,0:T(8,128)} %all-gather.17.cloned.1.call-done), kind=kLoop, calls=%fused_computation.3 | loop fusion | bytes 8388608 | tf_op jit(solution)/shard_map/squeeze | solution.py:214
  247.5 31.8 %all-gather.15.cloned.1.call-done = f32[4,1,64,32,128]{4,3,2,1,0:T(8,128)} async-done(((f32[1,1,64,32,128]{4,3,2,1,0:T(8,128)}), f32[4,1,64,32,128]{4,3,2,1,0:T(8,128)}) %all-gather.15.cloned.1.call-update) | async-done | bytes 4194320 | tf_op jit(solution)/shard_map/all_gather | solution.py:213
  279.3 4.2 %slice_bitcast_fusion.2 = (f32[64,32,128]{2,1,0:T(8,128)}, f32[64,32,128]{2,1,0:T(8,128)}, f32[64,32,128]{2,1,0:T(8,128)}, f32[64,32,128]{2,1,0:T(8,128)}) fusion(f32[4,1,64,32,128]{4,3,2,1,0:T(8,128)} %all-gather.15.cloned.1.call-done), kind=kLoop, calls=%fused_computation.4 | loop fusion | bytes 8388608 | tf_op jit(solution)/shard_map/squeeze | solution.py:214
  283.5 31.7 %all-gather.13.cloned.1.call-done = f32[4,1,64,32,128]{4,3,2,1,0:T(8,128)} async-done(((f32[1,1,64,32,128]{4,3,2,1,0:T(8,128)}), f32[4,1,64,32,128]{4,3,2,1,0:T(8,128)}) %all-gather.13.cloned.1.call-update) | async-done | bytes 4194320 | tf_op jit(solution)/shard_map/all_gather | solution.py:213
  315.2 4.2 %slice_bitcast_fusion.3 = (f32[64,32,128]{2,1,0:T(8,128)}, f32[64,32,128]{2,1,0:T(8,128)}, f32[64,32,128]{2,1,0:T(8,128)}, f32[64,32,128]{2,1,0:T(8,128)}) fusion(f32[4,1,64,32,128]{4,3,2,1,0:T(8,128)} %all-gather.13.cloned.1.call-done), kind=kLoop, calls=%fused_computation.5 | loop fusion | bytes 8388608 | tf_op jit(solution)/shard_map/squeeze | solution.py:214
  319.4 43.7 %correlate.1 = f32[32,2,256,128]{3,2,1,0:T(8,128)} custom-call(s32[11]{0:T(128)} %concatenate.3.meta, f32[64,32,128]{2,1,0:T(8,128)} %get-tuple-element.24.refs_0_, f32[64,32,128]{2,1,0:T(8,128)} %get-tuple-element.20.refs_1_, f32[64,32,128]{2,1,0:T(8,128)} %get-tuple-element.16.refs_2_, f32[64,32,128]{2,1,0:T(8,128)} %get-tuple-element.12.refs_3_, ...), custom_call_target="tpu_custom_call" | custom-call | tf_op jit(solution)/shard_map/correlate/pallas_call | solution.py:170
  (16 shorter events, 0.4 us)
Async XLA Ops:
  6.5 161.3 %all-gather.11.cloned.1.call-start = ((), (), s32[]{:S(2)}) async-start(), calls=%async_computation | async-start | bytes 10485760 | tf_op jit(solution)/shard_map/all_gather | solution.py:207
  11.2 5.3 %collective-permute-start = (f32[64,32,128]{2,1,0:T(8,128)}, f32[64,32,128]{2,1,0:T(8,128)S(1)}, u32[]{:S(2)}, u32[]{:S(2)}) collective-permute-start(f32[64,32,128]{2,1,0:T(8,128)} %whiten.3), channel_id=1, source_target_pairs={{0,1},{1,0},{2,3},{3,2},{4,5},{5,4},{6,7},{7,6},{8,9},{9,8},{10,11... | collective-permute-start | bytes 3145736 | tf_op jit(solution)/shard_map/ppermute | solution.py:200
  11.9 7.5 %copy-start.1 = (s32[6,2]{0,1:T(2,128)S(1)}, s32[6,2]{0,1:T(2,128)}, u32[]{:S(2)}) copy-start(s32[6,2]{0,1:T(2,128)} %param.6) | copy-start | bytes 148
  11.9 7.6 %copy-start = (s32[4,2]{0,1:T(2,128)S(1)}, s32[4,2]{0,1:T(2,128)}, u32[]{:S(2)}) copy-start(s32[4,2]{0,1:T(2,128)} %param.7) | copy-start | bytes 100
  19.3 188.0 %all-gather.19.cloned.1.call-start = ((), (), s32[]{:S(2)}) async-start(), calls=%async_computation.4 | async-start | bytes 5242880 | tf_op jit(solution)/shard_map/all_gather | solution.py:213
  172.1 71.2 %all-gather.17.cloned.1.call-start = ((), (), s32[]{:S(2)}) async-start(), calls=%async_computation.3 | async-start | bytes 5242880 | tf_op jit(solution)/shard_map/all_gather | solution.py:213
  172.9 106.4 %all-gather.15.cloned.1.call-start = ((), (), s32[]{:S(2)}) async-start(), calls=%async_computation.2 | async-start | bytes 5242880 | tf_op jit(solution)/shard_map/all_gather | solution.py:213
  173.5 141.8 %all-gather.13.cloned.1.call-start = ((), (), s32[]{:S(2)}) async-start(), calls=%async_computation.1 | async-start | bytes 5242880 | tf_op jit(solution)/shard_map/all_gather | solution.py:213
Sparse Core Ops, SparseCore 0:
  19.4 148.3 all-gather.10
  172.3 34.9 all-gather.18
  208.9 34.4 all-gather.16
  244.8 34.4 all-gather.14
  280.7 34.4 all-gather.12
